TPU v7x, 32 devices: a whole 2x2x4 slice. The times are simulated.
32 devices in a mesh: ty: 4 (over y, core), tx: 8 (over z, x).
Axes of the slice: x: 2, y: 2, z: 4, core: 2. Of those that a mesh axis runs over, the one named last changes fastest.
Arguments:
- object_re: float32 [2048, 4096], P('ty', 'tx'), may hold values from 0.5 to 1.5
- object_im: float32 [2048, 4096], P('ty', 'tx'), may hold values from -3 to 3
- probe_re: float32 [8, 128, 128], replicated, may hold values from -2 to 2
- probe_im: float32 [8, 128, 128], replicated, may hold values from -2 to 2
- patterns: float32 [4, 8, 16, 128, 128], P('ty', 'tx'), may hold values from 0.05 to 8
- offsets: int32 [4, 8, 16, 2], P('ty', 'tx'), may hold values from 0 to 511, as said below
- counts: int32 [4, 8, 8], P('ty', 'tx'), may hold values from 0 to 2, as said below
Outputs:
- new_object_re: float32 [2048, 4096], P('ty', 'tx')
- new_object_im: float32 [2048, 4096], P('ty', 'tx')
- new_probe_re: float32 [8, 128, 128], replicated
- new_probe_im: float32 [8, 128, 128], replicated
Inputs may be any that keep to these rules, and one draw needn't show every extreme that they name: Row offsets are below 512, column offsets below 512. `counts`: in every draw some reader receives 2 live scans from every owner tile of its row.
All inputs are finite; a program needn't handle non-finite values.
Results may differ from a plain program's by a relative error of at most 0.0001.
Values sent between devices are 32-bit elements; how exact they have to be, the bound alone decides.
A program may use at most 128 MiB of HBM per device.

v0:
```python
import math

import jax
import jax.numpy as jnp
from jax import lax
from jax.sharding import PartitionSpec as P


def from_behind(value, axis, steps):
    count = lax.axis_size(axis)
    first, last = (max(0, -steps), min(count, count - steps))
    return lax.ppermute(value, axis, [(source, source + steps) for source in range(first, last)])


def dft_tables(extent):
    indices = jnp.arange(extent, dtype=jnp.int32)
    phase_index = indices[:, None] * indices[None, :] % extent
    angles = phase_index.astype(jnp.float32) * (-2.0 * math.pi / extent)
    norm_scale = 1.0 / math.sqrt(extent)
    return (jnp.cos(angles) * norm_scale, jnp.sin(angles) * norm_scale)


def left_apply(cos_table, sin_table, plus_table, real_part, imag_part):
    high = lax.Precision.HIGHEST
    first_part = jnp.einsum("kn,bnc->bkc", cos_table, real_part, precision=high)
    second_part = jnp.einsum("kn,bnc->bkc", sin_table, imag_part, precision=high)
    third_part = jnp.einsum("kn,bnc->bkc", plus_table, real_part + imag_part, precision=high)
    return (first_part - second_part, third_part - first_part - second_part)


def right_apply(cos_table, sin_table, plus_table, real_part, imag_part):
    high = lax.Precision.HIGHEST
    first_part = jnp.einsum("bnc,ck->bnk", real_part, cos_table, precision=high)
    second_part = jnp.einsum("bnc,ck->bnk", imag_part, sin_table, precision=high)
    third_part = jnp.einsum("bnc,ck->bnk", real_part + imag_part, plus_table, precision=high)
    return (first_part - second_part, third_part - first_part - second_part)


def transform(tables, real_part, imag_part, direction_sign):
    cos_table, sin_table = tables
    sin_used = sin_table * direction_sign
    plus_table = cos_table + sin_used
    mid_real, mid_imag = left_apply(cos_table, sin_used, plus_table, real_part, imag_part)
    return right_apply(cos_table, sin_used, plus_table, mid_real, mid_imag)


def residuals(tables, probe_real, probe_imag, patch_real, patch_imag, measured):
    slot_total, extent = (patch_real.shape[0], patch_real.shape[1])
    modes = probe_real.shape[0]
    group_size = 4

    def in_groups(values):
        return values.reshape(slot_total // group_size, group_size, extent, extent)

    def visit_block(running, element):
        block_real, block_imag, intensity = element
        exit_real = probe_real[None] * block_real[:, None] - probe_imag[None] * block_imag[:, None]
        exit_imag = probe_real[None] * block_imag[:, None] + probe_imag[None] * block_real[:, None]
        far_real, far_imag = transform(
            tables,
            exit_real.reshape(-1, extent, extent),
            exit_imag.reshape(-1, extent, extent),
            1.0,
        )
        far_real = far_real.reshape(group_size, modes, extent, extent)
        far_imag = far_imag.reshape(group_size, modes, extent, extent)
        total_power = jnp.sum(far_real * far_real + far_imag * far_imag, axis=1)
        factor = (jnp.sqrt(intensity) / jnp.sqrt(jnp.maximum(total_power, 1.0)) - 1.0)[:, None]
        chi_real, chi_imag = transform(
            tables,
            (far_real * factor).reshape(-1, extent, extent),
            (far_imag * factor).reshape(-1, extent, extent),
            -1.0,
        )
        chi_real = chi_real.reshape(group_size, modes, extent, extent)
        chi_imag = chi_imag.reshape(group_size, modes, extent, extent)
        update_real = jnp.sum(probe_real[None] * chi_real + probe_imag[None] * chi_imag, axis=1)
        update_imag = jnp.sum(probe_real[None] * chi_imag - probe_imag[None] * chi_real, axis=1)
        grad_real = running[0] + jnp.sum(
            block_real[:, None] * chi_real + block_imag[:, None] * chi_imag, axis=0
        )
        grad_imag = running[1] + jnp.sum(
            block_real[:, None] * chi_imag - block_imag[:, None] * chi_real, axis=0
        )
        object_norm = running[2] + jnp.sum(
            block_real * block_real + block_imag * block_imag, axis=0
        )
        return ((grad_real, grad_imag, object_norm), (update_real, update_imag))

    modal = jnp.zeros((modes, extent, extent), jnp.float32)
    initial = (modal, modal, jnp.zeros((extent, extent), jnp.float32))
    sums, updates = lax.scan(
        visit_block, initial, (in_groups(patch_real), in_groups(patch_imag), in_groups(measured))
    )
    update_real = updates[0].reshape(slot_total, extent, extent)
    update_imag = updates[1].reshape(slot_total, extent, extent)
    return (update_real, update_imag, sums[0], sums[1], sums[2])


def cut_patches(extended_real, extended_imag, corners, alive_flags, extent):

    def cut_single(corner_pair, alive_flag):
        first_cut = lax.dynamic_slice(
            extended_real, (corner_pair[0], corner_pair[1]), (extent, extent)
        )
        second_cut = lax.dynamic_slice(
            extended_imag, (corner_pair[0], corner_pair[1]), (extent, extent)
        )
        return (first_cut * alive_flag, second_cut * alive_flag)

    return jax.vmap(cut_single)(corners, alive_flags)


def accumulate(update_real, update_imag, corners, alive_flags, probe_power, rows_total, cols_total):
    slot_total, extent = (update_real.shape[0], update_real.shape[1])
    zeros_tile = jnp.zeros((rows_total, cols_total), jnp.float32)

    def add_single(slot_index, running):
        corner = (corners[slot_index, 0], corners[slot_index, 1])

        def place_add(target, piece_add):
            current = lax.dynamic_slice(target, corner, (extent, extent))
            return lax.dynamic_update_slice(target, current + piece_add, corner)

        return (
            place_add(running[0], update_real[slot_index]),
            place_add(running[1], update_imag[slot_index]),
            place_add(running[2], probe_power * alive_flags[slot_index]),
        )

    return lax.fori_loop(0, slot_total, add_single, (zeros_tile, zeros_tile, zeros_tile))


def body(object_re, object_im, probe_re, probe_im, patterns, offsets, counts):
    height, tile_width = object_re.shape
    extent = probe_re.shape[1]
    slot_total = patterns.shape[2]
    capacity = slot_total // lax.axis_size("tx")
    measured = patterns[0, 0]
    corners = offsets[0, 0]
    slot_ids = jnp.arange(slot_total, dtype=jnp.int32)
    alive_flags = (slot_ids % capacity < counts[0, 0][slot_ids // capacity]).astype(jnp.float32)
    tables = dft_tables(extent)
    measured = lax.all_to_all(measured, "tx", split_axis=0, concat_axis=0, tiled=True)
    object_real, object_imag = (object_re, object_im)
    probe_real, probe_imag = (probe_re, probe_im)
    right_rim = from_behind((object_real[:, :extent], object_imag[:, :extent]), "tx", -1)
    wide_real = jnp.concatenate([object_real, right_rim[0]], axis=1)
    wide_imag = jnp.concatenate([object_imag, right_rim[1]], axis=1)
    lower_rim = from_behind((wide_real[:extent], wide_imag[:extent]), "ty", -1)
    extended_real = jnp.concatenate([wide_real, lower_rim[0]], axis=0)
    extended_imag = jnp.concatenate([wide_imag, lower_rim[1]], axis=0)
    patch_real, patch_imag = cut_patches(extended_real, extended_imag, corners, alive_flags, extent)
    update_real, update_imag, grad_real, grad_imag, object_norm = residuals(
        tables, probe_real, probe_imag, patch_real, patch_imag, measured
    )
    probe_power = jnp.sum(probe_real * probe_real + probe_imag * probe_imag, axis=0)
    numer_real, numer_imag, illumination = accumulate(
        update_real,
        update_imag,
        corners,
        alive_flags,
        probe_power,
        height + extent,
        tile_width + extent,
    )
    below = from_behind((numer_real[height:], numer_imag[height:], illumination[height:]), "ty", 1)
    upper_real = numer_real[:height].at[:extent].add(below[0])
    upper_imag = numer_imag[:height].at[:extent].add(below[1])
    upper_illum = illumination[:height].at[:extent].add(below[2])
    beside = from_behind(
        (upper_real[:, tile_width:], upper_imag[:, tile_width:], upper_illum[:, tile_width:]),
        "tx",
        1,
    )
    final_real = upper_real[:, :tile_width].at[:, :extent].add(beside[0])
    final_imag = upper_imag[:, :tile_width].at[:, :extent].add(beside[1])
    final_illum = upper_illum[:, :tile_width].at[:, :extent].add(beside[2])
    denominator = final_illum + 0.1 * jnp.max(probe_power)
    object_real = object_real + final_real / denominator
    object_imag = object_imag + final_imag / denominator
    summed = lax.psum((grad_real, grad_imag, object_norm), ("ty", "tx"))
    probe_real = probe_real + summed[0] / (summed[2] + 1.0)
    probe_imag = probe_imag + summed[1] / (summed[2] + 1.0)
    return (object_real, object_imag, probe_real, probe_imag)


def solution(mesh):
    return jax.shard_map(
        body,
        mesh=mesh,
        in_specs=(
            P("ty", "tx"),
            P("ty", "tx"),
            P(),
            P(),
            P("ty", "tx", None, None, None),
            P("ty", "tx", None, None),
            P("ty", "tx", None),
        ),
        out_specs=(P("ty", "tx"), P("ty", "tx"), P(), P()),
        check_vma=False,
    )
```

profile of v0, /device:TPU:0, one launch (start us, length us, event | category | flops | bytes accessed | tf_op | source)
XLA Modules:
  0.0 790.9 jit_solution(16059364084698533815)
XLA Ops:
  12.5 10.4 %all-to-all-start = ((f32[16,128,128]{2,1,0:T(8,128)}), f32[16,128,128]{2,1,0:T(8,128)}, u32[]{:S(2)}, u32[]{:S(2)}) async-start(f32[16,128,128]{2,1,0:T(8,128)} %bitcast.257), calls=%async_computation | async-start | bytes 2097152 | tf_op jit(solution)/shard_map/all_to_all | solution.py:144
  30.2 46.5 %while.48 = (s32[]{:T(128)}, f32[640,640]{1,0:T(8,128)}, s32[16,2]{0,1:T(2,128)S(1)}, f32[16,128,128]{2,1,0:T(8,128)S(1)}, s32[]{:T(128)}) while((s32[]{:T(128)}, f32[640,640]{1,0:T(8,128)}, s32[16,2]{0,1:T(2,128)S(1)}, f32[16,128,128]{2,1,0:T(8,128)S(1)}, s32[]{:T(128)}) %tuple.154), condition=%wide.while_cond.6, body=%wide.while_body.6.sunk | while | flops 2 | bytes 131181 | solution.py:103
  78.1 45.1 %while.49 = (s32[]{:T(128)}, f32[640,640]{1,0:T(8,128)}, s32[16,2]{0,1:T(2,128)S(1)}, f32[16,128,128]{2,1,0:T(8,128)S(1)}, s32[]{:T(128)}) while((s32[]{:T(128)}, f32[640,640]{1,0:T(8,128)}, s32[16,2]{0,1:T(2,128)S(1)}, f32[16,128,128]{2,1,0:T(8,128)S(1)}, s32[]{:T(128)}) %tuple.168), condition=%wide.while_cond.7, body=%wide.while_body.7.sunk | while | flops 2 | bytes 131181 | solution.py:106
  125.0 254.7 %while.50 = (s32[]{:T(128)}, f32[8,128,128]{2,1,0:T(8,128)}, f32[8,128,128]{2,1,0:T(8,128)}, f32[128,128]{1,0:T(8,128)S(1)}, f32[4,4,128,128]{3,2,1,0:T(8,128)},...) while((s32[]{:T(128)}, f32[8,128,128]{2,1,0:T(8,128)}, ...), condition=%wide.region_7.8_spmd.clone.clone, body=%wide.region_0.7_spmd.clone.clone.sunk | while | flops 9691381760 | bytes 156238768 | solution.py:92
  145.3 4.2 fusion.204
  149.4 3.8 fusion.202
  153.2 4.0 bitcast_reduce_fusion.2
  160.1 5.3 fusion.206
  172.8 3.8 fusion.210
  180.2 4.2 subtract_reduce_fusion.4
  208.2 3.8 fusion.204
  212.0 3.8 fusion.202
  215.8 4.0 bitcast_reduce_fusion.2
  222.7 5.4 fusion.206
  235.4 4.0 fusion.210
  243.0 4.2 subtract_reduce_fusion.4
  270.8 4.0 fusion.204
  274.8 3.8 fusion.202
  278.5 4.0 bitcast_reduce_fusion.2
  285.4 5.3 fusion.206
  290.8 3.7 fusion.207
  298.1 3.8 fusion.210
  305.5 4.2 subtract_reduce_fusion.4
  333.6 3.8 fusion.204
  337.3 3.8 fusion.202
  341.1 4.0 bitcast_reduce_fusion.2
  348.0 5.4 fusion.206
  360.7 4.0 fusion.210
  368.3 4.2 subtract_reduce_fusion.4
  380.3 136.5 %all-reduce.3.cloned.1.call-done = (f32[8,128,128]{2,1,0:T(8,128)}, f32[128,128]{1,0:T(8,128)}, f32[8,128,128]{2,1,0:T(8,128)}) async-done(((f32[8,128,128]{2,1,0:T(8,128)}, f32[128,128]{1,0:T(8,128)}, f32[8,128,128]{2,1,0:T(8,128)}), (f32[8,128,128]{2,1,0:T(8,128)}, f32[128,128]{1,0:T(8,128)}, f32[8,128,128]{2,1,0:T(8,128)})) %all-reduce.3.cloned.1.call-update) | async-done | bytes 1114128 | tf_op jit(solution)/shard_map/psum | solution.py:182
  521.6 219.0 %while.47 = (s32[]{:T(128)}, f32[640,640]{1,0:T(8,128)S(1)}, f32[640,640]{1,0:T(8,128)}, f32[640,640]{1,0:T(8,128)S(1)}, s32[16,2]{0,1:T(2,128)S(1)}, /*index=5*...) while((s32[]{:T(128)}, f32[640,640]{1,0:T(8,128)S(1)}, ...), condition=%wide.region_10.11_spmd, body=%wide.region_9.10_spmd.sunk | while | flops 65544 | bytes 983293 | solution.py:131
  741.4 5.2 collective-permute-start.4
  (445 shorter events, 455.2 us)
Async XLA Ops:
  7.2 16.0 %copy-start = (s32[1,1,8]{2,1,0:T(1,128)S(1)}, s32[1,1,8]{2,1,0:T(1,128)}, u32[]{:S(2)}) copy-start(s32[1,1,8]{2,1,0:T(1,128)} %param.29) | copy-start | bytes 100
  7.2 15.8 %copy-start.17 = (f32[512,512]{1,0:T(8,128)S(1)}, f32[512,512]{1,0:T(8,128)}, u32[]{:S(2)}) copy-start(f32[512,512]{1,0:T(8,128)} %param.23) | copy-start | bytes 3145732
  8.3 17.0 %collective-permute-start = (f32[512,128]{1,0:T(8,128)S(1)}, f32[512,128]{1,0:T(8,128)S(1)}, u32[]{:S(2)}, u32[]{:S(2)}) collective-permute-start(f32[512,128]{1,0:T(8,128)S(1)} %slice.176), channel_id=1, source_target_pairs={{1,0},{2,1},{3,2},{4,3},{5,4},{6,5},{7,6},{9,8},{10,9},{11,10},{12... | collective-permute-start | bytes 786440 | tf_op jit(solution)/shard_map/ppermute | solution.py:12
  11.2 15.4 %collective-permute-start.2 = (f32[512,128]{1,0:T(8,128)}, f32[512,128]{1,0:T(8,128)S(1)}, u32[]{:S(2)}, u32[]{:S(2)}) collective-permute-start(f32[512,128]{1,0:T(8,128)} %slice.180), channel_id=1, source_target_pairs={{1,0},{2,1},{3,2},{4,3},{5,4},{6,5},{7,6},{9,8},{10,9},{11,10},{12... | collective-permute-start | bytes 786440 | tf_op jit(solution)/shard_map/ppermute | solution.py:12
  12.5 10.6 %copy-start.20 = (s32[1,1,16,2]{2,3,1,0:T(2,128)S(1)}, s32[1,1,16,2]{2,3,1,0:T(2,128)}, u32[]{:S(2)}) copy-start(s32[1,1,16,2]{2,3,1,0:T(2,128)} %param.28) | copy-start | bytes 388
  12.5 112.4 %all-to-all-start = ((f32[16,128,128]{2,1,0:T(8,128)}), f32[16,128,128]{2,1,0:T(8,128)}, u32[]{:S(2)}, u32[]{:S(2)}) async-start(f32[16,128,128]{2,1,0:T(8,128)} %bitcast.257), calls=%async_computation | async-start | bytes 2097152 | tf_op jit(solution)/shard_map/all_to_all | solution.py:144
  22.9 493.9 %all-reduce.3.cloned.1.call-start = ((), (), s32[]{:S(2)}) async-start(), calls=%async_computation.1 | async-start | bytes 2228224 | tf_op jit(solution)/shard_map/psum | solution.py:182
  23.8 3.6 copy-start.22
  25.3 3.5 collective-permute-start.1
  27.4 49.3 %collective-permute-start.3 = (f32[128,640]{1,0:T(8,128)}, f32[128,640]{1,0:T(8,128)S(1)}, u32[]{:S(2)}, u32[]{:S(2)}) collective-permute-start(f32[128,640]{1,0:T(8,128)} %slice.225), channel_id=1, source_target_pairs={{8,0},{16,8},{24,16},{9,1},{17,9},{25,17},{10,2},{18,10},{26,18},{... | collective-permute-start | bytes 983048 | tf_op jit(solution)/shard_map/ppermute | solution.py:12
  124.9 255.3 %copy-start.23 = (s32[16]{0:T(128)S(1)}, s32[16]{0:T(128)}, u32[]{:S(2)}) copy-start(s32[16]{0:T(128)} %copy-done.22) | copy-start | bytes 196
  133.0 2.9 copy-start.2
  165.4 3.7 copy-start.3
  180.2 5.1 copy-start.7
  195.9 2.9 copy-start.2
  228.0 3.7 copy-start.3
  243.0 5.1 copy-start.7
  290.8 3.7 copy-start.3
  305.5 5.1 copy-start.7
  353.3 3.7 copy-start.3
  368.3 5.1 copy-start.7
  741.4 17.5 %collective-permute-start.4 = (f32[128,640]{1,0:T(8,128)}, f32[128,640]{1,0:T(8,128)}, u32[]{:S(2)}, u32[]{:S(2)}) collective-permute-start(f32[128,640]{1,0:T(8,128)} %slice.184), channel_id=1, source_target_pairs={{0,8},{8,16},{16,24},{1,9},{9,17},{17,25},{2,10},{10,18},{18,26},{... | collective-permute-start | bytes 983048 | tf_op jit(solution)/shard_map/ppermute | solution.py:12
  747.4 17.7 %collective-permute-start.6 = (f32[128,640]{1,0:T(8,128)}, f32[128,640]{1,0:T(8,128)}, u32[]{:S(2)}, u32[]{:S(2)}) collective-permute-start(f32[128,640]{1,0:T(8,128)} %slice.190), channel_id=1, source_target_pairs={{0,8},{8,16},{16,24},{1,9},{9,17},{17,25},{2,10},{10,18},{18,26},{... | collective-permute-start | bytes 983048 | tf_op jit(solution)/shard_map/ppermute | solution.py:12
  754.4 16.2 %collective-permute-start.8 = (f32[128,640]{1,0:T(8,128)}, f32[128,640]{1,0:T(8,128)}, u32[]{:S(2)}, u32[]{:S(2)}) collective-permute-start(f32[128,640]{1,0:T(8,128)} %slice.196), channel_id=1, source_target_pairs={{0,8},{8,16},{16,24},{1,9},{9,17},{17,25},{2,10},{10,18},{18,26},{... | collective-permute-start | bytes 983048 | tf_op jit(solution)/shard_map/ppermute | solution.py:12
  758.9 11.7 %copy-start.13 = (f32[512,640]{1,0:T(8,128)S(1)}, f32[512,640]{1,0:T(8,128)}, u32[]{:S(2)}) copy-start(f32[512,640]{1,0:T(8,128)} %slice.194) | copy-start | bytes 3932164
  760.8 10.9 %copy-start.15 = (f32[512,640]{1,0:T(8,128)S(1)}, f32[512,640]{1,0:T(8,128)}, u32[]{:S(2)}) copy-start(f32[512,640]{1,0:T(8,128)} %add_dynamic-update-slice_fusion.2) | copy-start | bytes 3932164
  761.9 13.5 %collective-permute-start.5 = (f32[512,128]{1,0:T(8,128)S(1)}, f32[512,128]{1,0:T(8,128)S(1)}, u32[]{:S(2)}, u32[]{:S(2)}) collective-permute-start(f32[512,128]{1,0:T(8,128)S(1)} %slice.228), channel_id=1, source_target_pairs={{0,1},{1,2},{2,3},{3,4},{4,5},{5,6},{6,7},{8,9},{9,10},{10,11},{11... | collective-permute-start | bytes 786440 | tf_op jit(solution)/shard_map/ppermute | solution.py:12
  766.8 5.0 copy-start.14
  767.9 9.4 %collective-permute-start.7 = (f32[512,128]{1,0:T(8,128)S(1)}, f32[512,128]{1,0:T(8,128)S(1)}, u32[]{:S(2)}, u32[]{:S(2)}) collective-permute-start(f32[512,128]{1,0:T(8,128)S(1)} %slice.231), channel_id=1, source_target_pairs={{0,1},{1,2},{2,3},{3,4},{4,5},{5,6},{6,7},{8,9},{9,10},{10,11},{11... | collective-permute-start | bytes 786440 | tf_op jit(solution)/shard_map/ppermute | solution.py:12
  772.0 9.9 %copy-start.16 = (f32[512,512]{1,0:T(8,128)S(1)}, f32[512,512]{1,0:T(8,128)}, u32[]{:S(2)}) copy-start(f32[512,512]{1,0:T(8,128)} %param.24) | copy-start | bytes 3145732
  772.0 9.9 %copy-start.18 = (f32[512,512]{1,0:T(8,128)S(1)}, f32[512,512]{1,0:T(8,128)}, u32[]{:S(2)}) copy-start(f32[512,512]{1,0:T(8,128)} %param.23) | copy-start | bytes 3145732
  772.2 9.0 %collective-permute-start.9 = (f32[512,128]{1,0:T(8,128)S(1)}, f32[512,128]{1,0:T(8,128)S(1)}, u32[]{:S(2)}, u32[]{:S(2)}) collective-permute-start(f32[512,128]{1,0:T(8,128)S(1)} %slice.234), channel_id=1, source_target_pairs={{0,1},{1,2},{2,3},{3,4},{4,5},{5,6},{6,7},{8,9},{9,10},{10,11},{11... | collective-permute-start | bytes 786440 | tf_op jit(solution)/shard_map/ppermute | solution.py:12
  (28 other events, 40.1 us)
Sparse Core Ops, SparseCore 0:
  380.4 136.3 all-reduce.2
where the time goes:
time: 800 us; the launch traced here: 791 us
  local copies, waits for them, and re-layouts  269 us (34%)
  matrix products  182 us (23%)
  waiting for transfers between devices  141 us (18%)
  other arithmetic  84.1 us (11%)
  loops' own time  64 us (8%)
  starting transfers between devices  35.1 us (4%)
  between operations  15.4 us (2%)
    psum x1, waiting for transfers between devices, body(): summed = lax.psum((grad_real, grad_imag, object_norm), ('ty', 'tx'))  137 us
    dynamic_update_slice x48, local copies, waits for them, and re-layouts, place_add(): return lax.dynamic_update_slice(target, current + piece_add, corner)  114 us
    gather x96, local copies, waits for them, and re-layouts  90.9 us
    another operation x1, loops' own time, accumulate(): lax.fori_loop(0, slot_total, add_single, (zeros_tile, zeros_tile, zeros_t...  57.7 us
    dot_general x8, matrix products, left_apply(): jnp.einsum('kn,bnc->bkc', sin_table, imag_part, precision=high)  36 us
    dot_general x8, matrix products, right_apply(): jnp.einsum('bnc,ck->bnk', real_part + imag_part, plus_table, precision=high)  32.8 us
    dot_general x8, matrix products, right_apply(): jnp.einsum('bnc,ck->bnk', imag_part, sin_table, precision=high)  31.1 us
    dot_general x8, matrix products, right_apply(): first_part = jnp.einsum('bnc,ck->bnk', real_part, cos_table, precision=high)  29.5 us
  transfers between devices with their start and end apart: 12, of which 4 were waited for; matrix products, arithmetic and copies ran while one was open for 15% of the time, Pallas kernels for 0%

commit v1 on v0

v1 whole, which is shorter than its diff:
```python
import math

import jax
import jax.numpy as jnp
import ml_dtypes
import numpy as np
from jax import lax
from jax.experimental import pallas as pl
from jax.experimental.pallas import tpu as pltpu
from jax.sharding import PartitionSpec as P

BF16 = jnp.bfloat16
F32 = jnp.float32
LANES = 128


def from_behind(value, axis, steps):
    count = lax.axis_size(axis)
    first, last = (max(0, -steps), min(count, count - steps))
    return lax.ppermute(value, axis, [(source, source + steps) for source in range(first, last)])


def dft_tables(extent):
    k = np.arange(extent)
    angle = (k[:, None] * k[None, :] % extent) * (-2.0 * math.pi / extent)
    cos, sin = np.cos(angle) / math.sqrt(extent), np.sin(angle) / math.sqrt(extent)
    table = np.block([[cos, sin], [-sin, cos]])

    def parts(values):
        high = values.astype(np.float32).astype(ml_dtypes.bfloat16)
        low = (values - high.astype(np.float64)).astype(np.float32).astype(ml_dtypes.bfloat16)
        return high, low

    high, low = parts(table)
    flip_high, flip_low = parts(table.T)
    return (
        np.concatenate([high, high, low], axis=0),
        np.concatenate([flip_high, flip_high, flip_low], axis=1),
        np.concatenate([high, high, low], axis=1),
        np.concatenate([flip_high, flip_high, flip_low], axis=0),
    )


def split(value):
    high = value.astype(BF16)
    low = (value - high.astype(F32)).astype(BF16)
    return high, low


def right_product(real, imag, table):
    rh, rl = split(real)
    ih, il = split(imag)
    lhs = jnp.concatenate([rh, ih, rl, il, rh, ih], axis=1)
    return jnp.dot(lhs, table, preferred_element_type=F32)


def left_product(table, real, imag):
    rh, rl = split(real)
    ih, il = split(imag)
    rhs = jnp.concatenate([rh, ih, rl, il, rh, ih], axis=0)
    return jnp.dot(table, rhs, preferred_element_type=F32)


def main_kernel(
    offsets, counts, wide_re, wide_im, probe_re, probe_im, measured,
    right_fwd, left_fwd, left_inv, right_inv,
    numer_re, numer_im, illum, grads,
    patch, power, far, update,
):
    slots, extent = measured.shape[0], measured.shape[1]
    modes = probe_re.shape[0]
    capacity = slots // counts.shape[0]
    numer_re[...] = jnp.zeros_like(numer_re)
    numer_im[...] = jnp.zeros_like(numer_im)
    illum[...] = jnp.zeros_like(illum)
    grads[...] = jnp.zeros_like(grads)
    lane = lax.broadcasted_iota(jnp.int32, (extent, LANES), 1)
    summed = probe_re[0] * probe_re[0] + probe_im[0] * probe_im[0]
    for m in range(1, modes):
        summed = summed + probe_re[m] * probe_re[m] + probe_im[m] * probe_im[m]
    power[...] = summed

    def visit(slot, carry):
        alive = slot % capacity < counts[slot // capacity]

        @pl.when(alive)
        def _():
            row = offsets[slot, 0]
            col = offsets[slot, 1]
            block = col // LANES
            inner = col % LANES
            rows = pl.ds(row, extent)
            back = lax.rem(LANES - inner, LANES)

            def cut(wide):
                first = pltpu.roll(wide[block, rows, :], back, 1)
                second = pltpu.roll(wide[block + 1, rows, :], back, 1)
                return jnp.where(lane < LANES - inner, first, second)

            patch[0] = cut(wide_re)
            patch[1] = cut(wide_im)
            total = jnp.zeros((extent, extent), F32)
            for m in range(0, modes, 2):
                mids = []
                for n in (m, m + 1):
                    a, b = patch[0], patch[1]
                    p, q = probe_re[n], probe_im[n]
                    mids.append(right_product(p * a - q * b, p * b + q * a, right_fwd[...]))
                wide_real = jnp.concatenate([y[:, :extent] for y in mids], axis=1)
                wide_imag = jnp.concatenate([y[:, extent:] for y in mids], axis=1)
                z = left_product(left_fwd[...], wide_real, wide_imag)
                far[m // 2] = z
                s = z[:extent] * z[:extent] + z[extent:] * z[extent:]
                total = total + s[:, :extent] + s[:, extent:]
            factor = jnp.sqrt(measured[slot]) / jnp.sqrt(jnp.maximum(total, 1.0)) - 1.0
            both = jnp.concatenate([factor, factor], axis=1)
            up_re = jnp.zeros((extent, extent), F32)
            up_im = jnp.zeros((extent, extent), F32)
            for m in range(0, modes, 2):
                z = far[m // 2]
                g = left_product(left_inv[...], z[:extent] * both, z[extent:] * both)
                for n in (m, m + 1):
                    cut_n = slice((n - m) * extent, (n - m + 1) * extent)
                    chi = right_product(g[:extent, cut_n], g[extent:, cut_n], right_inv[...])
                    c, d = chi[:, :extent], chi[:, extent:]
                    a, b = patch[0], patch[1]
                    p, q = probe_re[n], probe_im[n]
                    up_re = up_re + p * c + q * d
                    up_im = up_im + p * d - q * c
                    grads[n] += a * c + b * d
                    grads[modes + n] += a * d - b * c
            a, b = patch[0], patch[1]
            grads[2 * modes] += a * a + b * b

            def place(target, piece):
                moved = pltpu.roll(piece, inner, 1)
                target[block, rows, :] += jnp.where(lane >= inner, moved, 0.0)
                target[block + 1, rows, :] += jnp.where(lane < inner, moved, 0.0)

            place(numer_re, up_re)
            place(numer_im, up_im)
            place(illum, power[...])

        return carry

    lax.fori_loop(0, slots, visit, 0)


def local_work(offsets, counts, wide_re, wide_im, probe_re, probe_im, measured):
    modes, extent = probe_re.shape[0], probe_re.shape[1]
    tables = dft_tables(extent)
    vmem = pl.BlockSpec(memory_space=pltpu.VMEM)
    smem = pl.BlockSpec(memory_space=pltpu.SMEM)
    plane = jax.ShapeDtypeStruct(wide_re.shape, F32)
    return pl.pallas_call(
        main_kernel,
        out_shape=(plane, plane, plane, jax.ShapeDtypeStruct((2 * modes + 1, extent, extent), F32)),
        in_specs=[smem, smem] + [vmem] * 9,
        out_specs=(vmem,) * 4,
        scratch_shapes=[
            pltpu.VMEM((2, extent, extent), F32),
            pltpu.VMEM((extent, extent), F32),
            pltpu.VMEM((modes // 2, 2 * extent, 2 * extent), F32),
            pltpu.VMEM((2, extent, extent), F32),
        ],
        compiler_params=pltpu.CompilerParams(vmem_limit_bytes=48 * 1024 * 1024),
        name="local_work",
    )(offsets, counts, wide_re, wide_im, probe_re, probe_im, measured, *tables)


def blocked(value):
    rows, cols = value.shape
    return value.reshape(rows, cols // LANES, LANES).transpose(1, 0, 2)


def unblocked(value):
    blocks, rows, lanes = value.shape
    return value.transpose(1, 0, 2).reshape(rows, blocks * lanes)


def body(object_re, object_im, probe_re, probe_im, patterns, offsets, counts):
    height, tile_width = object_re.shape
    extent = probe_re.shape[1]
    measured = lax.all_to_all(patterns[0, 0], "tx", split_axis=0, concat_axis=0, tiled=True)
    right_rim = from_behind((object_re[:, :extent], object_im[:, :extent]), "tx", -1)
    wide_real = jnp.concatenate([object_re, right_rim[0]], axis=1)
    wide_imag = jnp.concatenate([object_im, right_rim[1]], axis=1)
    lower_rim = from_behind((wide_real[:extent], wide_imag[:extent]), "ty", -1)
    extended_real = jnp.concatenate([wide_real, lower_rim[0]], axis=0)
    extended_imag = jnp.concatenate([wide_imag, lower_rim[1]], axis=0)
    numer_real, numer_imag, illumination, grads = local_work(
        offsets[0, 0], counts[0, 0], blocked(extended_real), blocked(extended_imag),
        probe_re, probe_im, measured,
    )
    numer_real, numer_imag, illumination = (
        unblocked(numer_real), unblocked(numer_imag), unblocked(illumination)
    )
    probe_power = jnp.sum(probe_re * probe_re + probe_im * probe_im, axis=0)
    below = from_behind((numer_real[height:], numer_imag[height:], illumination[height:]), "ty", 1)
    upper_real = numer_real[:height].at[:extent].add(below[0])
    upper_imag = numer_imag[:height].at[:extent].add(below[1])
    upper_illum = illumination[:height].at[:extent].add(below[2])
    beside = from_behind(
        (upper_real[:, tile_width:], upper_imag[:, tile_width:], upper_illum[:, tile_width:]),
        "tx",
        1,
    )
    final_real = upper_real[:, :tile_width].at[:, :extent].add(beside[0])
    final_imag = upper_imag[:, :tile_width].at[:, :extent].add(beside[1])
    final_illum = upper_illum[:, :tile_width].at[:, :extent].add(beside[2])
    denominator = final_illum + 0.1 * jnp.max(probe_power)
    object_re = object_re + final_real / denominator
    object_im = object_im + final_imag / denominator
    summed = lax.psum(grads, ("ty", "tx"))
    modes = probe_re.shape[0]
    norm = summed[2 * modes] + 1.0
    probe_re = probe_re + summed[:modes] / norm
    probe_im = probe_im + summed[modes : 2 * modes] / norm
    return (object_re, object_im, probe_re, probe_im)


def solution(mesh):
    return jax.shard_map(
        body,
        mesh=mesh,
        in_specs=(
            P("ty", "tx"),
            P("ty", "tx"),
            P(),
            P(),
            P("ty", "tx", None, None, None),
            P("ty", "tx", None, None),
            P("ty", "tx", None),
        ),
        out_specs=(P("ty", "tx"), P("ty", "tx"), P(), P()),
        check_vma=False,
    )
```

time: 800 us -> 292 us (0.36)
  local copies, waits for them, and re-layouts: 269 us -> 40 us
  matrix products: 182 us -> 0 us
  loops' own time: 64 us -> 0 us
  other arithmetic: 84.1 us -> 26.1 us
  starting transfers between devices: 35.1 us -> 68.6 us
  Pallas kernels: 0 us -> 17.3 us
  waiting for transfers between devices: 141 us -> 124 us
    dot_general x48 -> x0, matrix products: 182 us -> none  [the longest x8 36 us: left_apply(): jnp.einsum('kn,bnc->bkc', sin_table, imag_part, precision=high)]
    dynamic_update_slice x52 -> x0, local copies, waits for them, and re-layouts: 117 us -> none  [the longest x48 114 us: place_add(): return lax.dynamic_update_slice(target, current + piece_add, corner)]
    gather x98 -> x0, local copies, waits for them, and re-layouts: 91.7 us -> none
    another operation x4 -> x0, loops' own time: 64 us -> none  [the longest x1 57.7 us: accumulate(): lax.fori_loop(0, slot_total, add_single, (zeros_tile, zeros_tile, zeros_t...]
    add x47 -> x2, other arithmetic: 45.6 us -> 5.8 us  [the longest x1 3.45 us: body(): object_im = object_im + final_imag / denominator]
    ppermute x10, starting transfers between devices: 24.7 us -> 61.1 us  [from_behind(): lax.ppermute(value, axis, [(source, source + steps) for source in range(f...]
    psum x1, waiting for transfers between devices: 137 us -> 107 us  [body(): summed = lax.psum(grads, ('ty', 'tx'))]
    dynamic_slice x32 -> x0, local copies, waits for them, and re-layouts: 19.1 us -> none  [the longest x16 9.59 us: add_single(): alive_flags[slot_index]]
  transfers between devices with their start and end apart: 12 -> 12, of which waited for: 4 -> 3; matrix products, arithmetic and copies ran while one was open for 15% -> 18% of each run, Pallas kernels for 0% -> 0%
where the time goes in v1:
time: 292 us; the launch traced here: 291 us
  waiting for transfers between devices  124 us (42%)
  starting transfers between devices  68.6 us (23%)
  local copies, waits for them, and re-layouts  40 us (14%)
  other arithmetic  26.1 us (9%)
  Pallas kernels  17.3 us (6%)
  between operations  15 us (5%)
    psum x1, waiting for transfers between devices, body(): summed = lax.psum(grads, ('ty', 'tx'))  107 us
    ppermute x10, starting transfers between devices, from_behind(): lax.ppermute(value, axis, [(source, source + steps) for source in range(f...  61.1 us
    pallas_call x1, Pallas kernels, local_work(): pl.pallas_call(main_kernel, out_shape=(plane, plane, plane, jax.ShapeDtyp...  17.3 us
    ppermute x10, waiting for transfers between devices, from_behind(): lax.ppermute(value, axis, [(source, source + steps) for source in range(f...  16.5 us
    unnamed x44, local copies, waits for them, and re-layouts  7.81 us
    all_to_all x1, starting transfers between devices, body(): lax.all_to_all(patterns[0, 0], 'tx', split_axis=0, concat_axis=0, tiled=T...  7.4 us
    another operation x6, local copies, waits for them, and re-layouts  6.04 us
  transfers between devices with their start and end apart: 12, of which 3 were waited for; matrix products, arithmetic and copies ran while one was open for 18% of the time, Pallas kernels for 0%

profile of v1, /device:TPU:0, one launch (start us, length us, event | category | flops | bytes accessed | tf_op | source)
XLA Modules:
  0.0 290.5 jit_solution(7989927537794070332)
XLA Ops:
  7.2 7.4 %all-to-all-start = ((f32[16,128,128]{2,1,0:T(8,128)}), f32[16,128,128]{2,1,0:T(8,128)S(1)}, u32[]{:S(2)}, u32[]{:S(2)}) async-start(f32[16,128,128]{2,1,0:T(8,128)} %bitcast.38), calls=%async_computation | async-start | bytes 2097152 | tf_op jit(solution)/shard_map/all_to_all | solution.py:184
  17.0 1.6 copy.49
  18.6 1.4 collective-permute-start
  20.1 13.8 %collective-permute-done.2 = f32[512,128]{0,1:T(8,128)} collective-permute-done((f32[512,128]{0,1:T(8,128)}, f32[512,128]{0,1:T(8,128)}, u32[]{:S(2)}, u32[]{:S(2)}) %collective-permute-start.2) | collective-permute-done | bytes 262176 | tf_op jit(solution)/shard_map/ppermute | solution.py:20
  33.9 1.6 pad_maximum_fusion.2
  36.8 2.6 collective-permute-done
  42.3 2.3 pad_maximum_fusion.1
  44.6 2.7 copy.41
  47.4 2.3 pad_maximum_fusion
  49.7 2.9 %copy.38 = f32[640,5,128]{2,0,1:T(8,128)} copy(f32[640,5,128]{0,2,1:T(8,128)} %bitcast.28) | data formatting | bytes 3276800 | tf_op jit(solution)/shard_map/reshape | solution.py:173
  53.7 17.3 %local_work.1 = (f32[5,640,128]{2,1,0:T(8,128)}, f32[5,640,128]{2,1,0:T(8,128)}, f32[5,640,128]{2,1,0:T(8,128)}, f32[17,128,128]{2,1,0:T(8,128)}) custom-call(s32[16,2]{1,0:T(8,128)S(1)} %copy.42.offsets, s32[8]{0:T(128)S(1)} %bitcast.24, f32[5,640,128]{2,1,0:T(8,128)} %bitcast.26, f32[5,640,128]{2,1,0:T(8,128)} %bitcast.25, f32[8,128,128]{2,1,0:T(8,128)S(1)} %copy-done, ...), custom_call_target="tpu_custom_call" | custom-call | tf_op jit(solution)/shard_map/local_work/pallas_call | solution.py:155
  73.0 16.4 %collective-permute-start.4 = (f32[128,640]{0,1:T(8,128)}, f32[128,640]{0,1:T(8,128)}, u32[]{:S(2)}, u32[]{:S(2)}) collective-permute-start(f32[128,640]{0,1:T(8,128)} %bitcast.10), channel_id=1, source_target_pairs={{0,8},{8,16},{16,24},{1,9},{9,17},{17,25},{2,10},{10,18},{18,26},{... | collective-permute-start | bytes 983048 | tf_op jit(solution)/shard_map/ppermute | solution.py:20
  91.4 8.3 %collective-permute-start.6 = (f32[128,640]{0,1:T(8,128)}, f32[128,640]{0,1:T(8,128)}, u32[]{:S(2)}, u32[]{:S(2)}) collective-permute-start(f32[128,640]{0,1:T(8,128)} %bitcast.14), channel_id=1, source_target_pairs={{0,8},{8,16},{16,24},{1,9},{9,17},{17,25},{2,10},{10,18},{18,26},{... | collective-permute-start | bytes 983048 | tf_op jit(solution)/shard_map/ppermute | solution.py:20
  99.7 1.8 fusion.6
  101.6 1.5 slice.231
  107.4 1.5 copy.43
  109.7 1.8 copy.46
  111.7 3.1 %collective-permute-start.8 = (f32[128,640]{0,1:T(8,128)S(1)}, f32[128,640]{0,1:T(8,128)}, u32[]{:S(2)}, u32[]{:S(2)}) collective-permute-start(f32[128,640]{0,1:T(8,128)S(1)} %bitcast.39), channel_id=1, source_target_pairs={{0,8},{8,16},{16,24},{1,9},{9,17},{17,25},{2,10},{10,18},{18,26},{... | collective-permute-start | bytes 983048 | tf_op jit(solution)/shard_map/ppermute | solution.py:20
  115.0 2.8 copy.50
  117.8 1.8 constant_dynamic-update-slice_fusion.2
  119.6 2.3 slice.234
  122.0 1.7 slice.236
  129.4 11.7 %collective-permute-start.5 = (f32[512,128]{0,1:T(8,128)}, f32[512,128]{0,1:T(8,128)}, u32[]{:S(2)}, u32[]{:S(2)}) collective-permute-start(f32[512,128]{0,1:T(8,128)} %slice.236), channel_id=1, source_target_pairs={{0,1},{1,2},{2,3},{3,4},{4,5},{5,6},{6,7},{8,9},{9,10},{10,11},{11... | collective-permute-start | bytes 786440 | tf_op jit(solution)/shard_map/ppermute | solution.py:20
  141.1 7.3 %collective-permute-start.7 = (f32[512,128]{0,1:T(8,128)}, f32[512,128]{0,1:T(8,128)}, u32[]{:S(2)}, u32[]{:S(2)}) collective-permute-start(f32[512,128]{0,1:T(8,128)} %slice.242), channel_id=1, source_target_pairs={{0,1},{1,2},{2,3},{3,4},{4,5},{5,6},{6,7},{8,9},{9,10},{10,11},{11... | collective-permute-start | bytes 786440 | tf_op jit(solution)/shard_map/ppermute | solution.py:20
  148.4 9.1 %collective-permute-start.9 = (f32[512,128]{0,1:T(8,128)}, f32[512,128]{0,1:T(8,128)}, u32[]{:S(2)}, u32[]{:S(2)}) collective-permute-start(f32[512,128]{0,1:T(8,128)} %slice.248), channel_id=1, source_target_pairs={{0,1},{1,2},{2,3},{3,4},{4,5},{5,6},{6,7},{8,9},{9,10},{10,11},{11... | collective-permute-start | bytes 786440 | tf_op jit(solution)/shard_map/ppermute | solution.py:20
  157.4 107.1 %all-reduce.2.cloned.1.call-done = f32[17,128,128]{2,1,0:T(8,128)} async-done(((f32[17,128,128]{2,1,0:T(8,128)}), f32[17,128,128]{2,1,0:T(8,128)}) %all-reduce.2.cloned.1.call-update) | async-done | bytes 1114128 | tf_op jit(solution)/shard_map/psum | solution.py:214
  265.4 2.4 fusion
  269.1 2.5 fusion.2
  271.6 2.4 fusion.3
  273.9 2.5 fusion.4
  276.4 3.4 %divide_add_fusion = (f32[512,512]{0,1:T(8,128)S(1)}, f32[512,512]{0,1:T(8,128)}) fusion(f32[512,512]{0,1:T(8,128)S(1)} %copy-done.8, f32[512,512]{0,1:T(8,128)} %fusion.4, f32[512,512]{0,1:T(8,128)} %fusion.3, f32[]{:T(128)S(6)} %mul_shard_map.3, f32[512,512]{0,1:T(8,128)S(1)} %copy-done.10, f32[512,512]{0,1:T(8,128)} %fusion.2), kind=kLoop, calls=%fused_computation.2 | loop fusion | flops 1310720 | bytes 7340036 | tf_op jit(solution)/shard_map/add | solution.py:213
  279.8 2.5 copy.54
  (79 shorter events, 25.7 us)
Async XLA Ops:
  7.2 7.5 %copy-start.18 = (f32[512,512]{1,0:T(8,128)S(1)}, f32[512,512]{1,0:T(8,128)}, u32[]{:S(2)}) copy-start(f32[512,512]{1,0:T(8,128)} %param.24) | copy-start | bytes 3145732
  7.2 45.4 %all-to-all-start = ((f32[16,128,128]{2,1,0:T(8,128)}), f32[16,128,128]{2,1,0:T(8,128)S(1)}, u32[]{:S(2)}, u32[]{:S(2)}) async-start(f32[16,128,128]{2,1,0:T(8,128)} %bitcast.38), calls=%async_computation | async-start | bytes 2097152 | tf_op jit(solution)/shard_map/all_to_all | solution.py:184
  14.6 249.9 %all-reduce.2.cloned.1.call-start = ((), (), s32[]{:S(2)}) async-start(), calls=%async_computation.1 | async-start | bytes 2228224 | tf_op jit(solution)/shard_map/psum | solution.py:214
  15.0 27.3 %copy-start.7 = (f32[512,512]{0,1:T(8,128)}, f32[512,512]{0,1:T(8,128)S(1)}, u32[]{:S(2)}) copy-start(f32[512,512]{0,1:T(8,128)S(1)} %copy.40) | copy-start | bytes 3145732
  15.7 18.2 %collective-permute-start.2 = (f32[512,128]{0,1:T(8,128)}, f32[512,128]{0,1:T(8,128)}, u32[]{:S(2)}, u32[]{:S(2)}) collective-permute-start(f32[512,128]{0,1:T(8,128)} %slice.230), channel_id=1, source_target_pairs={{1,0},{2,1},{3,2},{4,3},{5,4},{6,5},{7,6},{9,8},{10,9},{11,10},{12... | collective-permute-start | bytes 786440 | tf_op jit(solution)/shard_map/ppermute | solution.py:20
  18.6 28.8 %copy-start.9 = (f32[512,512]{0,1:T(8,128)}, f32[512,512]{0,1:T(8,128)S(1)}, u32[]{:S(2)}) copy-start(f32[512,512]{0,1:T(8,128)S(1)} %copy.49) | copy-start | bytes 3145732
  18.6 22.8 %copy-start.19 = (s32[1,1,16,2]{2,3,1,0:T(2,128)S(1)}, s32[1,1,16,2]{2,3,1,0:T(2,128)}, u32[]{:S(2)}) copy-start(s32[1,1,16,2]{2,3,1,0:T(2,128)} %param.28) | copy-start | bytes 388
  18.6 20.8 %collective-permute-start = (f32[512,128]{0,1:T(8,128)S(1)}, f32[512,128]{0,1:T(8,128)S(1)}, u32[]{:S(2)}, u32[]{:S(2)}) collective-permute-start(f32[512,128]{0,1:T(8,128)S(1)} %slice.229), channel_id=1, source_target_pairs={{1,0},{2,1},{3,2},{4,3},{5,4},{6,5},{7,6},{9,8},{10,9},{11,10},{12... | collective-permute-start | bytes 786440 | tf_op jit(solution)/shard_map/ppermute | solution.py:20
  35.5 6.8 %collective-permute-start.3 = (f32[128,640]{0,1:T(8,128)}, f32[128,640]{0,1:T(8,128)}, u32[]{:S(2)}, u32[]{:S(2)}) collective-permute-start(f32[128,640]{0,1:T(8,128)} %pad_maximum_fusion.2), channel_id=1, source_target_pairs={{8,0},{16,8},{24,16},{9,1},{17,9},{25,17},{10,2},{18,10},{26,18},{... | collective-permute-start | bytes 983048 | tf_op jit(solution)/shard_map/ppermute | solution.py:20
  40.2 7.2 %collective-permute-start.1 = (f32[128,640]{0,1:T(8,128)}, f32[128,640]{0,1:T(8,128)}, u32[]{:S(2)}, u32[]{:S(2)}) collective-permute-start(f32[128,640]{0,1:T(8,128)} %pad_maximum_fusion.3), channel_id=1, source_target_pairs={{8,0},{16,8},{24,16},{9,1},{17,9},{25,17},{10,2},{18,10},{26,18},{... | collective-permute-start | bytes 983048 | tf_op jit(solution)/shard_map/ppermute | solution.py:20
  49.6 3.0 %copy-start = (f32[8,128,128]{2,1,0:T(8,128)S(1)}, f32[8,128,128]{2,1,0:T(8,128)}, u32[]{:S(2)}) copy-start(f32[8,128,128]{2,1,0:T(8,128)} %probe_re.1) | copy-start | bytes 1572868
  49.6 3.0 %copy-start.1 = (f32[8,128,128]{2,1,0:T(8,128)S(1)}, f32[8,128,128]{2,1,0:T(8,128)}, u32[]{:S(2)}) copy-start(f32[8,128,128]{2,1,0:T(8,128)} %probe_im.1) | copy-start | bytes 1572868
  49.6 3.0 %copy-start.2 = (bf16[768,256]{1,0:T(8,128)(2,1)S(1)}, bf16[768,256]{1,0:T(8,128)(2,1)}, u32[]{:S(2)}) copy-start(bf16[768,256]{1,0:T(8,128)(2,1)} %constant.152.clone.right_fwd) | copy-start | bytes 1179652
  49.6 3.0 %copy-start.3 = (bf16[256,768]{1,0:T(8,128)(2,1)S(1)}, bf16[256,768]{1,0:T(8,128)(2,1)}, u32[]{:S(2)}) copy-start(bf16[256,768]{1,0:T(8,128)(2,1)} %constant.153.clone.left_fwd) | copy-start | bytes 1179652
  49.6 3.0 %copy-start.4 = (bf16[256,768]{1,0:T(8,128)(2,1)S(1)}, bf16[256,768]{1,0:T(8,128)(2,1)}, u32[]{:S(2)}) copy-start(bf16[256,768]{1,0:T(8,128)(2,1)} %constant.154.clone.left_inv) | copy-start | bytes 1179652
  49.7 3.0 %copy-start.6 = (s32[1,1,8]{2,1,0:T(1,128)S(1)}, s32[1,1,8]{2,1,0:T(1,128)}, u32[]{:S(2)}) copy-start(s32[1,1,8]{2,1,0:T(1,128)} %param.29) | copy-start | bytes 100
  52.7 1.0 copy-start.5
  73.0 44.8 %collective-permute-start.4 = (f32[128,640]{0,1:T(8,128)}, f32[128,640]{0,1:T(8,128)}, u32[]{:S(2)}, u32[]{:S(2)}) collective-permute-start(f32[128,640]{0,1:T(8,128)} %bitcast.10), channel_id=1, source_target_pairs={{0,8},{8,16},{16,24},{1,9},{9,17},{17,25},{2,10},{10,18},{18,26},{... | collective-permute-start | bytes 983048 | tf_op jit(solution)/shard_map/ppermute | solution.py:20
  91.4 32.2 %collective-permute-start.6 = (f32[128,640]{0,1:T(8,128)}, f32[128,640]{0,1:T(8,128)}, u32[]{:S(2)}, u32[]{:S(2)}) collective-permute-start(f32[128,640]{0,1:T(8,128)} %bitcast.14), channel_id=1, source_target_pairs={{0,8},{8,16},{16,24},{1,9},{9,17},{17,25},{2,10},{10,18},{18,26},{... | collective-permute-start | bytes 983048 | tf_op jit(solution)/shard_map/ppermute | solution.py:20
  101.5 1.8 copy-start.14
  103.4 1.9 copy-start.13
  109.7 1.8 copy-start.15
  111.7 14.8 %collective-permute-start.8 = (f32[128,640]{0,1:T(8,128)S(1)}, f32[128,640]{0,1:T(8,128)}, u32[]{:S(2)}, u32[]{:S(2)}) collective-permute-start(f32[128,640]{0,1:T(8,128)S(1)} %bitcast.39), channel_id=1, source_target_pairs={{0,8},{8,16},{16,24},{1,9},{9,17},{17,25},{2,10},{10,18},{18,26},{... | collective-permute-start | bytes 983048 | tf_op jit(solution)/shard_map/ppermute | solution.py:20
  114.9 2.9 copy-start.17
  119.6 4.0 %copy-start.16 = (f32[128,5,128]{0,2,1:T(8,128)S(1)}, f32[128,5,128]{0,2,1:T(8,128)}, u32[]{:S(2)}) copy-start(f32[128,5,128]{0,2,1:T(8,128)} %copy.47) | copy-start | bytes 983044
  124.7 1.8 copy-start.11
  127.5 1.9 copy-start.12
  129.4 139.7 %collective-permute-start.5 = (f32[512,128]{0,1:T(8,128)}, f32[512,128]{0,1:T(8,128)}, u32[]{:S(2)}, u32[]{:S(2)}) collective-permute-start(f32[512,128]{0,1:T(8,128)} %slice.236), channel_id=1, source_target_pairs={{0,1},{1,2},{2,3},{3,4},{4,5},{5,6},{6,7},{8,9},{9,10},{10,11},{11... | collective-permute-start | bytes 786440 | tf_op jit(solution)/shard_map/ppermute | solution.py:20
  141.1 130.5 %collective-permute-start.7 = (f32[512,128]{0,1:T(8,128)}, f32[512,128]{0,1:T(8,128)}, u32[]{:S(2)}, u32[]{:S(2)}) collective-permute-start(f32[512,128]{0,1:T(8,128)} %slice.242), channel_id=1, source_target_pairs={{0,1},{1,2},{2,3},{3,4},{4,5},{5,6},{6,7},{8,9},{9,10},{10,11},{11... | collective-permute-start | bytes 786440 | tf_op jit(solution)/shard_map/ppermute | solution.py:20
  148.4 125.6 %collective-permute-start.9 = (f32[512,128]{0,1:T(8,128)}, f32[512,128]{0,1:T(8,128)}, u32[]{:S(2)}, u32[]{:S(2)}) collective-permute-start(f32[512,128]{0,1:T(8,128)} %slice.248), channel_id=1, source_target_pairs={{0,1},{1,2},{2,3},{3,4},{4,5},{5,6},{6,7},{8,9},{9,10},{10,11},{11... | collective-permute-start | bytes 786440 | tf_op jit(solution)/shard_map/ppermute | solution.py:20
  267.7 8.7 %copy-start.8 = (f32[512,512]{0,1:T(8,128)S(1)}, f32[512,512]{0,1:T(8,128)}, u32[]{:S(2)}) copy-start(f32[512,512]{0,1:T(8,128)} %copy-done.7) | copy-start | bytes 3145732
  267.7 8.7 %copy-start.10 = (f32[512,512]{0,1:T(8,128)S(1)}, f32[512,512]{0,1:T(8,128)}, u32[]{:S(2)}) copy-start(f32[512,512]{0,1:T(8,128)} %copy-done.9) | copy-start | bytes 3145732
Sparse Core Ops, SparseCore 0:
  117.9 146.5 all-reduce.1
